TPU v7x, 512 devices: a whole 4x8x8 slice. The times are simulated.
512 devices in a mesh: seq: 128 (over z_lo, x, y), dp: 4 (over z_hi, core).
Axes of the slice: x: 4, y: 8, z: 8 (z_hi: 2, z_lo: 4; z = z_hi * 4 + z_lo), core: 2. Of those that a mesh axis runs over, the one named last changes fastest.
Arguments:
- byte_qkv: bfloat16 [4, 32768, 3072], P('dp', 'seq'), may hold values from -6 to 6
- patch_qkv: bfloat16 [4, 8192, 3072], P('dp', 'seq'), may hold values from -6 to 6
- patch_gain: float32 [3072], replicated, may hold values from 0.3 to 1.5
- out_grad: bfloat16 [4, 32768, 1024], P('dp', 'seq'), may hold values from -48 to 48
- patch_slot: int32 [4, 32768], P('dp', 'seq'), may hold values from 0 to 63, as said below
- lead: int32 [4, 128], P('dp', 'seq'), may hold values from 0 to 15, as said below
Outputs:
- byte_grad: bfloat16 [4, 32768, 3072], P('dp', 'seq')
- patch_grad: bfloat16 [4, 8192, 3072], P('dp', 'seq')
- gain_grad: float32 [3072], replicated
Inputs may be any that keep to these rules, and one draw needn't show every extreme that they name: Patches are runs of 1 to 31 bytes of a stream. A patch is owned by the device that holds its first byte; each device numbers the patches starting on it 0, 1, 2 and so on in order, and patch_slot gives each byte the number of its patch on the owning device. Every device holds the first byte of at least one patch. lead[s, d] bytes at the start of device d's run of stream s belong to the last patch that starts on device d - 1; lead[s, 0] = 0.
All inputs are finite; a program needn't handle non-finite values.
Results may differ from a plain program's by a relative error of at most 0.011.
Values may be sent and summed in bfloat16 or wider, within the bound.
A program may use at most 128 MiB of HBM per device.

v0:
```python
import math
import jax
import jax.numpy as jnp
from jax import lax
from jax.sharding import PartitionSpec as P

HEADS = 8
HEAD_DIM = 128
WIN = 512


def shifted(value, axis, steps):
    count = lax.axis_size(axis)
    initial, last = (max(0, -steps), min(count, count - steps))
    return lax.ppermute(value, axis, [(source, source + steps) for source in range(initial, last)])


def local(byte_qkv, patch_qkv, patch_gain, out_grad, patch_slot, lead):
    own_bytes = byte_qkv[0]
    patch_table = patch_qkv[0]
    cotangent = out_grad[0]
    slot_ids = patch_slot[0]
    row_count = own_bytes.shape[0]
    feature_count = cotangent.shape[1]
    capacity = patch_table.shape[0]
    first_pos = lax.axis_index("seq") * row_count
    reach_blocks = -(-WIN // row_count)
    inv_sqrt = 1.0 / math.sqrt(HEAD_DIM)
    local_rows = lax.broadcasted_iota(jnp.int32, (row_count,), 0)
    leading = local_rows < lead[0, 0]
    owned_slots = jnp.where(leading, -1, slot_ids)
    last_slot = jnp.max(owned_slots)
    last_row = lax.dynamic_slice_in_dim(patch_table, last_slot, 1, 0)
    prev_row = shifted(last_row, "seq", 1)
    slot_axis = lax.broadcasted_iota(jnp.int32, (row_count, capacity), 1)
    pick_rows = (slot_ids[:, None] == slot_axis).astype(jnp.bfloat16)
    patch_rows = jnp.dot(pick_rows, patch_table, preferred_element_type=jnp.float32)
    patch_rows = jnp.where(leading[:, None], prev_row.astype(jnp.float32), patch_rows)
    hidden = (patch_gain * patch_rows + own_bytes.astype(jnp.float32)).astype(jnp.bfloat16)
    queries = hidden[:, :feature_count]
    key_values = hidden[:, feature_count:]
    blocks = [key_values]
    arrived = shifted(key_values, "seq", 1)
    blocks.append(arrived)
    steps_back = 2
    arrived = shifted(key_values, "seq", steps_back)
    blocks.append(arrived)
    window = jnp.concatenate(blocks[::-1], axis=0)
    key_count = window.shape[0]
    query_pos = first_pos + local_rows
    key_pos = (
        first_pos - reach_blocks * row_count + lax.broadcasted_iota(jnp.int32, (key_count,), 0)
    )
    in_window = (
        (key_pos[None, :] <= query_pos[:, None])
        & (key_pos[None, :] > query_pos[:, None] - WIN)
        & (key_pos[None, :] >= 0)
    )
    query_parts = []
    key_parts = []
    value_parts = []
    max_list = []
    total_list = []
    delta_list = []
    for head_index in range(HEADS):
        low = head_index * HEAD_DIM
        query_head = queries[:, low : low + HEAD_DIM]
        cot_head = cotangent[:, low : low + HEAD_DIM]
        key_head = window[:, low : low + HEAD_DIM]
        value_head = window[:, feature_count + low : feature_count + low + HEAD_DIM]
        scores = (
            jnp.einsum("qe,ke->qk", query_head, key_head, preferred_element_type=jnp.float32)
            * inv_sqrt
        )
        scores = jnp.where(in_window, scores, -jnp.inf)
        row_max = jnp.max(scores, axis=1, keepdims=True)
        exponent = jnp.where(in_window, jnp.exp(scores - row_max), 0.0)
        row_total = jnp.sum(exponent, axis=1, keepdims=True)
        attn_prob = exponent / row_total
        prob_half = attn_prob.astype(jnp.bfloat16)
        value_parts.append(
            jnp.einsum("qk,qe->ke", prob_half, cot_head, preferred_element_type=jnp.float32)
        )
        prob_grad = jnp.einsum(
            "qe,ke->qk", cot_head, value_head, preferred_element_type=jnp.float32
        )
        row_delta = jnp.sum(attn_prob * prob_grad, axis=1, keepdims=True)
        score_grad = (attn_prob * (prob_grad - row_delta)).astype(jnp.bfloat16)
        query_parts.append(
            jnp.einsum("qk,ke->qe", score_grad, key_head, preferred_element_type=jnp.float32)
            * inv_sqrt
        )
        key_parts.append(
            jnp.einsum("qk,qe->ke", score_grad, query_head, preferred_element_type=jnp.float32)
            * inv_sqrt
        )
        max_list.append(row_max[:, 0])
        total_list.append(row_total[:, 0])
        delta_list.append(row_delta[:, 0])
    query_grad = jnp.concatenate(query_parts, axis=1)
    key_part = jnp.concatenate(key_parts, axis=1)
    value_part = jnp.concatenate(value_parts, axis=1)
    back_grads = jnp.concatenate([key_part, value_part], axis=1)
    own_grads = back_grads[key_count - row_count :]
    for steps_back in range(1, reach_blocks + 1):
        piece_first = (reach_blocks - steps_back) * row_count
        piece = back_grads[piece_first : piece_first + row_count]
        own_grads = own_grads + shifted(piece, "seq", -steps_back)
    hidden_grad = jnp.concatenate([query_grad, own_grads], axis=1)
    byte_grad = hidden_grad.astype(jnp.bfloat16)[None]
    lead_sum = jnp.sum(jnp.where(leading[:, None], hidden_grad, 0.0), axis=0, keepdims=True)
    from_next = shifted(lead_sum, "seq", -1)
    slot_column = lax.broadcasted_iota(jnp.int32, (capacity, row_count), 0)
    member = ((slot_ids[None, :] == slot_column) & jnp.logical_not(leading)[None, :]).astype(
        jnp.float32
    )
    slot_sums = jnp.dot(
        member, hidden_grad, precision=lax.Precision.HIGHEST, preferred_element_type=jnp.float32
    )
    slot_index = lax.broadcasted_iota(jnp.int32, (capacity, 1), 0)
    slot_sums = slot_sums + (slot_index == last_slot).astype(jnp.float32) * from_next
    patch_grad = (patch_gain * slot_sums).astype(jnp.bfloat16)[None]
    gain_term = jnp.sum(slot_sums * patch_table.astype(jnp.float32), axis=0)
    gain_grad = lax.psum(gain_term, ("seq", "dp")) / row_count
    return (byte_grad, patch_grad, gain_grad)


def solution(mesh):
    placed = (
        P("dp", "seq", None),
        P("dp", "seq", None),
        P(),
        P("dp", "seq", None),
        P("dp", "seq"),
        P("dp", "seq"),
    )
    return jax.shard_map(
        local,
        mesh=mesh,
        in_specs=placed,
        out_specs=(P("dp", "seq", None), P("dp", "seq", None), P()),
        check_vma=False,
    )
```

profile of v0, /device:TPU:1, one launch (start us, length us, event | category | flops | bytes accessed | tf_op | source)
XLA Modules:
  0.0 348.9 jit_solution(16617319942461404328)
XLA Ops:
  1.3 1.3 select_reduce_fusion.1
  4.5 0.8 dynamic-slice_bitcast_fusion
  5.4 4.0 %collective-permute-start = (bf16[1,3072]{1,0:T(2,128)(2,1)S(1)}, bf16[1,3072]{1,0:T(2,128)(2,1)S(1)}, u32[]{:S(2)}, u32[]{:S(2)}) collective-permute-start(bf16[1,3072]{1,0:T(2,128)(2,1)S(1)} %dynamic-slice_bitcast_fusion), channel_id=1, source_target_pairs={{0,4},{4,8},{8,12},{12,16},{16,20},{20,24},{24,28},{28,32},{32,36}... | collective-permute-start | bytes 18440 | tf_op jit(solution)/shard_map/ppermute | solution.py:15
  9.4 0.8 collective-permute-done
  10.2 2.3 fusion
  12.6 4.6 %collective-permute-start.2 = (bf16[256,2048]{1,0:T(8,128)(2,1)S(1)}, bf16[256,2048]{1,0:T(8,128)(2,1)}, u32[]{:S(2)}, u32[]{:S(2)}) collective-permute-start(bf16[256,2048]{1,0:T(8,128)(2,1)S(1)} %slice.154), channel_id=1, source_target_pairs={{0,4},{4,8},{8,12},{12,16},{16,20},{20,24},{24,28},{28,32},{32,36}... | collective-permute-start | bytes 3145736 | tf_op jit(solution)/shard_map/ppermute | solution.py:15
  17.2 5.1 %collective-permute-start.1 = (bf16[256,2048]{1,0:T(8,128)(2,1)S(1)}, bf16[256,2048]{1,0:T(8,128)(2,1)}, u32[]{:S(2)}, u32[]{:S(2)}) collective-permute-start(bf16[256,2048]{1,0:T(8,128)(2,1)S(1)} %slice.154), channel_id=1, source_target_pairs={{0,8},{4,12},{8,16},{12,20},{16,24},{20,28},{24,32},{28,36},{32,40... | collective-permute-start | bytes 3145736 | tf_op jit(solution)/shard_map/ppermute | solution.py:15
  22.3 0.6 compare_convert_fusion
  23.0 10.7 %collective-permute-done.2 = bf16[256,2048]{1,0:T(8,128)(2,1)} collective-permute-done((bf16[256,2048]{1,0:T(8,128)(2,1)S(1)}, bf16[256,2048]{1,0:T(8,128)(2,1)}, u32[]{:S(2)}, u32[]{:S(2)}) %collective-permute-start.2) | collective-permute-done | bytes 1048608 | tf_op jit(solution)/shard_map/ppermute | solution.py:15
  33.6 24.7 %collective-permute-done.1 = bf16[256,2048]{1,0:T(8,128)(2,1)} collective-permute-done((bf16[256,2048]{1,0:T(8,128)(2,1)S(1)}, bf16[256,2048]{1,0:T(8,128)(2,1)}, u32[]{:S(2)}, u32[]{:S(2)}) %collective-permute-start.1) | collective-permute-done | bytes 1048608 | tf_op jit(solution)/shard_map/ppermute | solution.py:15
  58.3 1.8 pad_maximum_fusion
  64.9 0.9 fusion.33
  65.8 1.4 multiply_reduce_fusion.1
  67.2 1.1 multiply_reduce_fusion.3
  68.3 1.1 multiply_reduce_fusion.2
  69.4 1.0 multiply_convert_fusion.6
  71.9 1.0 multiply_convert_fusion.1
  72.9 1.2 multiply_convert_fusion.3
  75.7 0.6 convolution_dynamic-update-slice_fusion.7
  76.9 0.6 convolution_dynamic-update-slice_fusion.5
  77.5 0.6 convolution_dynamic-update-slice_fusion.4
  79.3 0.6 convolution_dynamic-update-slice_fusion.1
  80.0 0.6 convolution_dynamic-update-slice_fusion
  81.1 1.3 collective-permute-start.4
  82.4 1.3 collective-permute-start.3
  85.6 29.1 %collective-permute-done.4 = f32[256,2048]{1,0:T(8,128)S(1)} collective-permute-done((f32[256,2048]{1,0:T(8,128)S(1)}, f32[256,2048]{1,0:T(8,128)S(1)}, u32[]{:S(2)}, u32[]{:S(2)}) %collective-permute-start.4) | collective-permute-done | bytes 2097184 | tf_op jit(solution)/shard_map/ppermute | solution.py:15
  114.7 46.9 %collective-permute-done.3 = f32[256,2048]{1,0:T(8,128)S(1)} collective-permute-done((f32[256,2048]{1,0:T(8,128)S(1)}, f32[256,2048]{1,0:T(8,128)S(1)}, u32[]{:S(2)}, u32[]{:S(2)}) %collective-permute-start.3) | collective-permute-done | bytes 2097184 | tf_op jit(solution)/shard_map/ppermute | solution.py:15
  161.7 0.6 constant_dynamic-update-slice_fusion.8
  162.7 1.3 collective-permute-start.5
  164.5 44.3 %collective-permute-done.5 = f32[1,3072]{1,0:T(1,128)S(1)} collective-permute-done((f32[1,3072]{1,0:T(1,128)S(1)}, f32[1,3072]{1,0:T(1,128)S(1)}, u32[]{:S(2)}, u32[]{:S(2)}) %collective-permute-start.5) | collective-permute-done | bytes 12320 | tf_op jit(solution)/shard_map/ppermute | solution.py:15
  208.9 2.2 multiply_reduce_fusion
  211.1 137.2 %psum.7 = f32[3072]{0:T(1024)S(1)} all-reduce(f32[3072]{0:T(1024)S(1)} %get-tuple-element.20), channel_id=1, replica_groups=mesh['seq'=128,'dp'=4] {'seq','dp'}, use_global_device_ids=true, to_apply=%region_27.28 | all-reduce | flops 3072 | bytes 24576 | tf_op jit(solution)/shard_map/psum | solution.py:124
  (60 shorter events, 13.5 us)
Async XLA Ops:
  5.4 4.9 %collective-permute-start = (bf16[1,3072]{1,0:T(2,128)(2,1)S(1)}, bf16[1,3072]{1,0:T(2,128)(2,1)S(1)}, u32[]{:S(2)}, u32[]{:S(2)}) collective-permute-start(bf16[1,3072]{1,0:T(2,128)(2,1)S(1)} %dynamic-slice_bitcast_fusion), channel_id=1, source_target_pairs={{0,4},{4,8},{8,12},{12,16},{16,20},{20,24},{24,28},{28,32},{32,36}... | collective-permute-start | bytes 18440 | tf_op jit(solution)/shard_map/ppermute | solution.py:15
  12.6 21.1 %collective-permute-start.2 = (bf16[256,2048]{1,0:T(8,128)(2,1)S(1)}, bf16[256,2048]{1,0:T(8,128)(2,1)}, u32[]{:S(2)}, u32[]{:S(2)}) collective-permute-start(bf16[256,2048]{1,0:T(8,128)(2,1)S(1)} %slice.154), channel_id=1, source_target_pairs={{0,4},{4,8},{8,12},{12,16},{16,20},{20,24},{24,28},{28,32},{32,36}... | collective-permute-start | bytes 3145736 | tf_op jit(solution)/shard_map/ppermute | solution.py:15
  17.2 41.1 %collective-permute-start.1 = (bf16[256,2048]{1,0:T(8,128)(2,1)S(1)}, bf16[256,2048]{1,0:T(8,128)(2,1)}, u32[]{:S(2)}, u32[]{:S(2)}) collective-permute-start(bf16[256,2048]{1,0:T(8,128)(2,1)S(1)} %slice.154), channel_id=1, source_target_pairs={{0,8},{4,12},{8,16},{12,20},{16,24},{20,28},{24,32},{28,36},{32,40... | collective-permute-start | bytes 3145736 | tf_op jit(solution)/shard_map/ppermute | solution.py:15
  62.0 1.8 copy-start.1
  81.1 33.7 %collective-permute-start.4 = (f32[256,2048]{1,0:T(8,128)S(1)}, f32[256,2048]{1,0:T(8,128)S(1)}, u32[]{:S(2)}, u32[]{:S(2)}) collective-permute-start(f32[256,2048]{1,0:T(8,128)S(1)} %get-tuple-element.19), channel_id=1, source_target_pairs={{8,0},{12,4},{16,8},{20,12},{24,16},{28,20},{32,24},{36,28},{40,32... | collective-permute-start | bytes 6291464 | tf_op jit(solution)/shard_map/ppermute | solution.py:15
  82.4 79.3 %collective-permute-start.3 = (f32[256,2048]{1,0:T(8,128)S(1)}, f32[256,2048]{1,0:T(8,128)S(1)}, u32[]{:S(2)}, u32[]{:S(2)}) collective-permute-start(f32[256,2048]{1,0:T(8,128)S(1)} %get-tuple-element.18), channel_id=1, source_target_pairs={{4,0},{8,4},{12,8},{16,12},{20,16},{24,20},{28,24},{32,28},{36,32}... | collective-permute-start | bytes 6291464 | tf_op jit(solution)/shard_map/ppermute | solution.py:15
  162.7 46.1 %collective-permute-start.5 = (f32[1,3072]{1,0:T(1,128)S(1)}, f32[1,3072]{1,0:T(1,128)S(1)}, u32[]{:S(2)}, u32[]{:S(2)}) collective-permute-start(f32[1,3072]{1,0:T(1,128)S(1)} %bitcast.89), channel_id=1, source_target_pairs={{4,0},{8,4},{12,8},{16,12},{20,16},{24,20},{28,24},{32,28},{36,32}... | collective-permute-start | bytes 36872 | tf_op jit(solution)/shard_map/ppermute | solution.py:15
  164.0 44.8 %copy-start = (bf16[1,64,3072]{2,1,0:T(8,128)(2,1)S(1)}, bf16[1,64,3072]{2,1,0:T(8,128)(2,1)}, u32[]{:S(2)}) copy-start(bf16[1,64,3072]{2,1,0:T(8,128)(2,1)} %param.7) | copy-start | bytes 1179652
  164.1 44.8 %copy-start.2 = (f32[3072]{0:T(1024)S(1)}, f32[3072]{0:T(1024)}, u32[]{:S(2)}) copy-start(f32[3072]{0:T(1024)} %param.8) | copy-start | bytes 36868
  164.1 44.8 %copy-start.3 = (s32[1,256]{1,0:T(1,128)S(1)}, s32[1,256]{1,0:T(1,128)}, u32[]{:S(2)}) copy-start(s32[1,256]{1,0:T(1,128)} %param.10) | copy-start | bytes 3076
  164.5 46.6 %copy-start.4 = (bf16[1,256,3072]{2,1,0:T(8,128)(2,1)}, bf16[1,256,3072]{2,1,0:T(8,128)(2,1)S(1)}, u32[]{:S(2)}) copy-start(bf16[1,256,3072]{2,1,0:T(8,128)(2,1)S(1)} %bitcast_dynamic-update-slice_fusion) | copy-start | bytes 4718596
where the time goes:
time: 349 us
  waiting for transfers between devices  157 us (45%)
  blocking collectives  137 us (39%)
  matrix products  23.3 us (7%)
  starting transfers between devices  17.6 us (5%)
  other arithmetic  9.05 us (3%)
  between operations  3.69 us (1%)
    ppermute x6, waiting for transfers between devices, shifted(): lax.ppermute(value, axis, [(source, source + steps) for source in range(i...  157 us
    psum x1, blocking collectives, local(): gain_grad = lax.psum(gain_term, ('seq', 'dp')) / row_count  137 us
    ppermute x6, starting transfers between devices, shifted(): lax.ppermute(value, axis, [(source, source + steps) for source in range(i...  17.6 us
  transfers between devices with their start and end apart: 6, of which 6 were waited for; matrix products, arithmetic and copies ran while one was open for 1% of the time, Pallas kernels for 0%

commit v1 on v0

--- a/solution.py
+++ b/solution.py
@@ -121,7 +121,7 @@
     slot_sums = slot_sums + (slot_index == last_slot).astype(jnp.float32) * from_next
     patch_grad = (patch_gain * slot_sums).astype(jnp.bfloat16)[None]
     gain_term = jnp.sum(slot_sums * patch_table.astype(jnp.float32), axis=0)
-    gain_grad = lax.psum(gain_term, ("seq", "dp")) / row_count
+    gain_grad = jnp.sum(lax.all_gather(gain_term, ("seq", "dp")), axis=0) / row_count
     return (byte_grad, patch_grad, gain_grad)
 
 

time: 349 us -> 1090 us (3.12)
  waiting for transfers between devices: 157 us -> 998 us
  blocking collectives: 137 us -> 0 us
  between operations: 3.69 us -> 17 us
    all_gather x0 -> x1, waiting for transfers between devices: none -> 845 us  [local(): lax.all_gather(gain_term, ('seq', 'dp'))]
    psum x1 -> x0, blocking collectives: 137 us -> none  [local(): gain_grad = lax.psum(gain_term, ('seq', 'dp')) / row_count]
  transfers between devices with their start and end apart: 6 -> 7, of which waited for: 6 -> 7; matrix products, arithmetic and copies ran while one was open for 1% -> 1% of each run, Pallas kernels for 0% -> 0%
where the time goes in v1:
time: 1090 us
  waiting for transfers between devices  998 us (92%)
  matrix products  28.7 us (3%)
  starting transfers between devices  17.6 us (2%)
  between operations  17 us (2%)
  other arithmetic  15.1 us (1%)
    all_gather x1, waiting for transfers between devices, local(): lax.all_gather(gain_term, ('seq', 'dp'))  845 us
    ppermute x6, waiting for transfers between devices, shifted(): lax.ppermute(value, axis, [(source, source + steps) for source in range(i...  153 us
  transfers between devices with their start and end apart: 7, of which 7 were waited for; matrix products, arithmetic and copies ran while one was open for 1% of the time, Pallas kernels for 0%

profile of v1, /device:TPU:1, one launch (start us, length us, event | category | flops | bytes accessed | tf_op | source)
XLA Modules:
  0.0 1085.3 jit_solution(13467128613789688987)
XLA Ops:
  7.9 1.3 select_reduce_fusion.1
  11.9 4.0 collective-permute-start
  16.8 2.3 fusion
  19.2 4.6 collective-permute-start.2
  23.8 5.1 collective-permute-start.1
  29.6 10.7 collective-permute-done.2
  40.2 24.5 %collective-permute-done.1 = bf16[256,2048]{1,0:T(8,128)(2,1)} collective-permute-done((bf16[256,2048]{1,0:T(8,128)(2,1)S(1)}, bf16[256,2048]{1,0:T(8,128)(2,1)}, u32[]{:S(2)}, u32[]{:S(2)}) %collective-permute-start.1) | collective-permute-done | bytes 1048608 | tf_op jit(solution)/shard_map/ppermute | solution.py:15
  64.8 1.7 pad_maximum_fusion
  72.1 1.4 multiply_reduce_fusion.1
  73.5 1.1 multiply_reduce_fusion.3
  74.6 1.1 multiply_reduce_fusion.2
  75.7 1.0 multiply_convert_fusion.6
  76.7 0.9 constant_dynamic-update-slice_fusion.7
  77.9 0.9 constant_dynamic-update-slice_fusion.6
  79.4 0.9 multiply_convert_fusion.1
  80.3 1.2 multiply_convert_fusion.3
  88.5 1.3 collective-permute-start.4
  89.8 1.3 collective-permute-start.3
  91.1 0.9 constant_dynamic-update-slice_fusion.5
  92.0 0.9 constant_dynamic-update-slice_fusion.4
  92.9 0.9 constant_dynamic-update-slice_fusion.3
  94.8 0.9 constant_dynamic-update-slice_fusion.1
  95.7 0.9 constant_dynamic-update-slice_fusion
  96.6 25.7 %collective-permute-done.4 = f32[256,2048]{1,0:T(8,128)S(1)} collective-permute-done((f32[256,2048]{1,0:T(8,128)S(1)}, f32[256,2048]{1,0:T(8,128)S(1)}, u32[]{:S(2)}, u32[]{:S(2)}) %collective-permute-start.4) | collective-permute-done | bytes 2097184 | tf_op jit(solution)/shard_map/ppermute | solution.py:15
  122.3 46.9 %collective-permute-done.3 = f32[256,2048]{1,0:T(8,128)S(1)} collective-permute-done((f32[256,2048]{1,0:T(8,128)S(1)}, f32[256,2048]{1,0:T(8,128)S(1)}, u32[]{:S(2)}, u32[]{:S(2)}) %collective-permute-start.3) | collective-permute-done | bytes 2097184 | tf_op jit(solution)/shard_map/ppermute | solution.py:15
  170.3 1.3 collective-permute-start.5
  171.6 44.8 %collective-permute-done.5 = f32[1,3072]{1,0:T(1,128)S(1)} collective-permute-done((f32[1,3072]{1,0:T(1,128)S(1)}, f32[1,3072]{1,0:T(1,128)S(1)}, u32[]{:S(2)}, u32[]{:S(2)}) %collective-permute-start.5) | collective-permute-done | bytes 12320 | tf_op jit(solution)/shard_map/ppermute | solution.py:15
  216.4 2.8 multiply_reduce_fusion
  219.3 3.6 bitcast_dynamic-update-slice_fusion
  222.9 844.8 %all-gather.3.cloned.1.call-done = f32[1572864]{0:T(1024)} async-done(((f32[3072]{0:T(1024)}), f32[1572864]{0:T(1024)}) %all-gather.3.cloned.1.call-update) | async-done | bytes 6291472 | tf_op jit(solution)/shard_map/all_gather | solution.py:124
  1067.6 7.1 reshape.198
  1074.8 3.1 reduce_sum.189
  (66 shorter events, 18.4 us)
Async XLA Ops:
  7.2 1060.5 %all-gather.3.cloned.1.call-start = ((), (), s32[]{:S(2)}) async-start(), calls=%async_computation | async-start | bytes 6303744 | tf_op jit(solution)/shard_map/all_gather | solution.py:124
  11.9 4.9 collective-permute-start
  19.2 21.1 %collective-permute-start.2 = (bf16[256,2048]{1,0:T(8,128)(2,1)S(1)}, bf16[256,2048]{1,0:T(8,128)(2,1)}, u32[]{:S(2)}, u32[]{:S(2)}) collective-permute-start(bf16[256,2048]{1,0:T(8,128)(2,1)S(1)} %slice.154), channel_id=1, source_target_pairs={{0,4},{4,8},{8,12},{12,16},{16,20},{20,24},{24,28},{28,32},{32,36}... | collective-permute-start | bytes 3145736 | tf_op jit(solution)/shard_map/ppermute | solution.py:15
  23.8 41.0 %collective-permute-start.1 = (bf16[256,2048]{1,0:T(8,128)(2,1)S(1)}, bf16[256,2048]{1,0:T(8,128)(2,1)}, u32[]{:S(2)}, u32[]{:S(2)}) collective-permute-start(bf16[256,2048]{1,0:T(8,128)(2,1)S(1)} %slice.154), channel_id=1, source_target_pairs={{0,8},{4,12},{8,16},{12,20},{16,24},{20,28},{24,32},{28,36},{32,40... | collective-permute-start | bytes 3145736 | tf_op jit(solution)/shard_map/ppermute | solution.py:15
  68.3 1.8 copy-start.3
  88.0 81.2 %copy-start = (f32[768,2048]{1,0:T(8,128)}, f32[768,2048]{1,0:T(8,128)S(1)}, u32[]{:S(2)}) copy-start(f32[768,2048]{1,0:T(8,128)S(1)} %convolution_dynamic-update-slice_fusion) | copy-start | bytes 18874372
  88.5 33.8 %collective-permute-start.4 = (f32[256,2048]{1,0:T(8,128)S(1)}, f32[256,2048]{1,0:T(8,128)S(1)}, u32[]{:S(2)}, u32[]{:S(2)}) collective-permute-start(f32[256,2048]{1,0:T(8,128)S(1)} %get-tuple-element.19), channel_id=1, source_target_pairs={{8,0},{12,4},{16,8},{20,12},{24,16},{28,20},{32,24},{36,28},{40,32... | collective-permute-start | bytes 6291464 | tf_op jit(solution)/shard_map/ppermute | solution.py:15
  89.8 79.4 %collective-permute-start.3 = (f32[256,2048]{1,0:T(8,128)S(1)}, f32[256,2048]{1,0:T(8,128)S(1)}, u32[]{:S(2)}, u32[]{:S(2)}) collective-permute-start(f32[256,2048]{1,0:T(8,128)S(1)} %get-tuple-element.18), channel_id=1, source_target_pairs={{4,0},{8,4},{12,8},{16,12},{20,16},{24,20},{28,24},{32,28},{36,32}... | collective-permute-start | bytes 6291464 | tf_op jit(solution)/shard_map/ppermute | solution.py:15
  169.2 50.0 %copy-start.1 = (f32[256,2048]{1,0:T(8,128)}, f32[256,2048]{1,0:T(8,128)S(1)}, u32[]{:S(2)}) copy-start(f32[256,2048]{1,0:T(8,128)S(1)} %collective-permute-done.3) | copy-start | bytes 6291460
  169.8 46.6 %copy-start.2 = (bf16[1,64,3072]{2,1,0:T(8,128)(2,1)S(1)}, bf16[1,64,3072]{2,1,0:T(8,128)(2,1)}, u32[]{:S(2)}) copy-start(bf16[1,64,3072]{2,1,0:T(8,128)(2,1)} %param.7) | copy-start | bytes 1179652
  169.9 46.6 %copy-start.4 = (f32[3072]{0:T(1024)S(1)}, f32[3072]{0:T(1024)}, u32[]{:S(2)}) copy-start(f32[3072]{0:T(1024)} %param.8) | copy-start | bytes 36868
  169.9 46.6 %copy-start.5 = (s32[1,256]{1,0:T(1,128)S(1)}, s32[1,256]{1,0:T(1,128)}, u32[]{:S(2)}) copy-start(s32[1,256]{1,0:T(1,128)} %param.10) | copy-start | bytes 3076
  170.3 46.1 %collective-permute-start.5 = (f32[1,3072]{1,0:T(1,128)S(1)}, f32[1,3072]{1,0:T(1,128)S(1)}, u32[]{:S(2)}, u32[]{:S(2)}) collective-permute-start(f32[1,3072]{1,0:T(1,128)S(1)} %bitcast.89), channel_id=1, source_target_pairs={{4,0},{8,4},{12,8},{16,12},{20,16},{24,20},{28,24},{32,28},{36,32}... | collective-permute-start | bytes 36872 | tf_op jit(solution)/shard_map/ppermute | solution.py:15
Sparse Core Ops, SparseCore 0:
  219.4 848.2 all-gather.2
